TPU v7x, 256 devices: a whole 4x4x8 slice. The times are simulated.
256 devices in a mesh: gx: 8 (over y, core), gy: 8 (over z_hi, x), af: 4 (over z_lo).
Axes of the slice: x: 4, y: 4, z: 8 (z_hi: 2, z_lo: 4; z = z_hi * 4 + z_lo), core: 2. Of those that a mesh axis runs over, the one named last changes fastest.
Arguments:
- volume: bfloat16 [32, 32, 128, 128], P('af', 'gx', 'gy'), may hold values from -6 to 6
- weight_one: bfloat16 [32, 32, 3, 3, 3], P('af'), may hold values from -0.21875 to 0.21875
- bias_one: float32 [32], P('af'), may hold values from -1 to 1
- weight_two: bfloat16 [32, 32, 3, 3, 3], P('af'), may hold values from -0.21875 to 0.21875
- cotangent: bfloat16 [32, 32, 128, 128], P('af', 'gx', 'gy'), may hold values from -6 to 6
Outputs:
- output: bfloat16 [32, 32, 128, 128], P('af', 'gx', 'gy')
- input_grad: bfloat16 [32, 32, 128, 128], P('af', 'gx', 'gy')
- grad_one: float32 [32, 32, 3, 3, 3], P('af')
- bias_grad: float32 [32], P('af')
- grad_two: float32 [32, 32, 3, 3, 3], P('af')
All inputs are finite; a program needn't handle non-finite values.
Results may differ from a plain program's by a relative error of at most 0.0065.
Values may be sent and summed in bfloat16 or wider, within the bound.
A program may use at most 64 MiB of HBM per device.

v0:
```python
import math
import jax
import jax.numpy as jnp
from jax import lax
from jax.sharding import PartitionSpec as P


def with_halo(cells, sides, width):
    for axis, dim in sides:
        count = lax.axis_size(axis)
        ends = count - 1
        head = lax.slice_in_dim(cells, 0, width, axis=dim)
        tail = lax.slice_in_dim(cells, cells.shape[dim] - width, cells.shape[dim], axis=dim)
        cells = jnp.concatenate(
            [
                lax.ppermute(tail, axis, [(i, (i + 1) % count) for i in range(ends)]),
                cells,
                lax.ppermute(head, axis, [((i + 1) % count, i) for i in range(ends)]),
            ],
            axis=dim,
        )
    return cells


def conv_valid(padded, weight):
    size_x = padded.shape[1] - 2
    size_y = padded.shape[2] - 2
    size_z = padded.shape[3] - 2
    total = jnp.zeros((weight.shape[0], size_x, size_y, size_z), jnp.float32)
    for off_x in range(3):
        for off_y in range(3):
            for off_z in range(3):
                window = padded[
                    :, off_x : off_x + size_x, off_y : off_y + size_y, off_z : off_z + size_z
                ]
                total = total + jnp.einsum(
                    "oi,ixyz->oxyz",
                    weight[:, :, off_x, off_y, off_z],
                    window,
                    preferred_element_type=jnp.float32,
                )
    return total


def kernel_grad(padded, cot_field):
    size_x = cot_field.shape[1]
    size_y = cot_field.shape[2]
    size_z = cot_field.shape[3]
    blocks = []
    for off_x in range(3):
        for off_y in range(3):
            for off_z in range(3):
                window = padded[
                    :, off_x : off_x + size_x, off_y : off_y + size_y, off_z : off_z + size_z
                ]
                blocks.append(
                    jnp.einsum(
                        "oxyz,ixyz->oi", cot_field, window, preferred_element_type=jnp.float32
                    )
                )
    stacked = jnp.stack(blocks, axis=-1)
    return stacked.reshape(cot_field.shape[0], padded.shape[0], 3, 3, 3)


def flipped(weight):
    return jnp.transpose(jnp.flip(weight, (2, 3, 4)), (1, 0, 2, 3, 4))


def depth_pad(values):
    return jnp.pad(values, ((0, 0), (0, 0), (0, 0), (1, 1)))


def full_padded(values):
    gathered = lax.all_gather(values, "af", axis=0, tiled=True)
    rimmed = with_halo(gathered, (("gx", 1), ("gy", 2)), 1)
    return depth_pad(rimmed)


def silu_grad(hidden_grad, pre_act):
    sigma_vals = jax.nn.sigmoid(pre_act)
    return (hidden_grad * sigma_vals * (1.0 + pre_act * (1.0 - sigma_vals))).astype(jnp.bfloat16)


def body(volume, weight_one, bias_one, weight_two, cotangent):
    own_rows = volume.shape[0]
    vol_pad = full_padded(volume)
    pre_act = conv_valid(vol_pad, weight_one) + bias_one[:, None, None, None]
    hidden = jax.nn.silu(pre_act).astype(jnp.bfloat16)
    hid_pad = full_padded(hidden)
    output = conv_valid(hid_pad, weight_two).astype(jnp.bfloat16)
    local_two = kernel_grad(hid_pad, cotangent)
    every_one, every_two = (
        lax.all_gather(weight_one, "af", axis=0, tiled=True),
        lax.all_gather(weight_two, "af", axis=0, tiled=True),
    )
    first_row = lax.axis_index("af") * own_rows

    def transposed(cot_field, every_w):
        padded = full_padded(cot_field)
        turned = lax.dynamic_slice_in_dim(flipped(every_w), first_row, own_rows, 0)
        return conv_valid(padded, turned)

    hidden_grad = transposed(cotangent, every_two)
    pre_grad = silu_grad(hidden_grad, pre_act)
    local_one = kernel_grad(vol_pad, pre_grad)
    local_bias = jnp.sum(pre_grad, axis=(1, 2, 3), dtype=jnp.float32)
    input_grad = transposed(pre_grad, every_one).astype(jnp.bfloat16)
    summed_one, summed_bias, summed_two = lax.psum((local_one, local_bias, local_two), ("gx", "gy"))
    cell_total = (
        volume.shape[1]
        * lax.axis_size("gx")
        * volume.shape[2]
        * lax.axis_size("gy")
        * volume.shape[3]
    )
    grad_scale = 1.0 / math.sqrt(cell_total)
    return (
        output,
        input_grad,
        summed_one * grad_scale,
        summed_bias * grad_scale,
        summed_two * grad_scale,
    )


def solution(mesh):
    return jax.shard_map(
        body,
        mesh=mesh,
        in_specs=(
            P("af", "gx", "gy", None),
            P("af", None, None, None, None),
            P("af"),
            P("af", None, None, None, None),
            P("af", "gx", "gy", None),
        ),
        out_specs=(
            P("af", "gx", "gy", None),
            P("af", "gx", "gy", None),
            P("af", None, None, None, None),
            P("af"),
            P("af", None, None, None, None),
        ),
        check_vma=False,
    )
```

profile of v0, /device:TPU:0, one launch (start us, length us, event | category | flops | bytes accessed | tf_op | source)
XLA Modules:
  0.0 645.6 jit_solution(11498958030644135914)
XLA Ops:
  0.6 1.0 copy.43
  1.7 14.6 %all_gather.18 = bf16[32,4,16,128]{3,0,2,1:T(8,128)(2,1)S(1)} all-gather(bf16[8,4,16,128]{3,0,2,1:T(8,128)(2,1)S(1)} %copy.43), channel_id=1, replica_groups=mesh['gx'=8,'gy'=8,'af'=4] {'af'}, dimensions={0}, use_global_device_ids=true | all-gather | bytes 655360 | tf_op jit(solution)/shard_map/all_gather | solution.py:74
  16.3 1.3 collective-permute-start
  17.6 1.3 collective-permute-start.1
  19.9 15.3 %all_gather.22 = bf16[32,4,16,128]{3,0,2,1:T(8,128)(2,1)S(1)} all-gather(bf16[8,4,16,128]{3,0,2,1:T(8,128)(2,1)S(1)} %copy.46), channel_id=1, replica_groups=mesh['gx'=8,'gy'=8,'af'=4] {'af'}, dimensions={0}, use_global_device_ids=true | all-gather | bytes 655360 | tf_op jit(solution)/shard_map/all_gather | solution.py:74
  35.2 2.1 collective-permute-start.8
  37.4 1.3 collective-permute-start.9
  38.9 13.0 %all_gather.21 = bf16[32,32,3,3,3]{1,0,4,3,2:T(8,128)(2,1)S(1)} all-gather(bf16[8,32,3,3,3]{1,0,4,3,2:T(8,128)(2,1)S(1)} %copy-done.48), channel_id=1, replica_groups=mesh['gx'=8,'gy'=8,'af'=4] {'af'}, dimensions={0}, use_global_device_ids=true | all-gather | bytes 69120 | tf_op jit(solution)/shard_map/all_gather | solution.py:94
  52.3 13.0 %all_gather.20 = bf16[32,32,3,3,3]{1,0,4,3,2:T(8,128)(2,1)S(1)} all-gather(bf16[8,32,3,3,3]{1,0,4,3,2:T(8,128)(2,1)S(1)} %copy-done.50), channel_id=1, replica_groups=mesh['gx'=8,'gy'=8,'af'=4] {'af'}, dimensions={0}, use_global_device_ids=true | all-gather | bytes 69120 | tf_op jit(solution)/shard_map/all_gather | solution.py:93
  66.0 3.4 collective-permute-start.2
  69.4 1.3 collective-permute-start.3
  71.2 4.5 collective-permute-start.10
  75.8 1.5 collective-permute-start.11
  92.0 15.4 %all_gather.23 = bf16[32,4,16,128]{3,0,2,1:T(8,128)(2,1)S(1)} all-gather(bf16[8,4,16,128]{3,0,2,1:T(8,128)(2,1)S(1)} %get-tuple-element.51), channel_id=1, replica_groups=mesh['gx'=8,'gy'=8,'af'=4] {'af'}, dimensions={0}, use_global_device_ids=true | all-gather | bytes 655360 | tf_op jit(solution)/shard_map/all_gather | solution.py:74
  107.4 14.4 %all_gather.19 = bf16[32,4,16,128]{3,0,2,1:T(8,128)(2,1)S(1)} all-gather(bf16[8,4,16,128]{3,0,2,1:T(8,128)(2,1)S(1)} %get-tuple-element.48), channel_id=1, replica_groups=mesh['gx'=8,'gy'=8,'af'=4] {'af'}, dimensions={0}, use_global_device_ids=true | all-gather | bytes 655360 | tf_op jit(solution)/shard_map/all_gather | solution.py:74
  122.7 1.3 collective-permute-start.4
  123.9 1.5 collective-permute-start.5
  132.2 8.9 %collective-permute-start.12 = (bf16[32,1,16,128]{3,0,2,1:T(8,128)(2,1)S(1)}, bf16[32,1,16,128]{3,0,2,1:T(8,128)(2,1)S(1)}, u32[]{:S(2)}, u32[]{:S(2)}) collective-permute-start(bf16[32,1,16,128]{3,0,2,1:T(8,128)(2,1)S(1)} %get-tuple-element.27), channel_id=1, source_target_pairs={{0,32},{32,64},{64,96},{96,128},{128,160},{160,192},{192,224},{1,3... | collective-permute-start | bytes 393224 | tf_op jit(solution)/shard_map/ppermute | solution.py:16
  141.1 1.3 collective-permute-start.13
  144.3 4.4 collective-permute-start.6
  148.7 1.3 collective-permute-start.7
  150.2 9.7 %collective-permute-start.14 = (bf16[32,6,1,128]{3,0,2,1:T(8,128)(2,1)S(1)}, bf16[32,6,1,128]{3,0,2,1:T(8,128)(2,1)S(1)}, u32[]{:S(2)}, u32[]{:S(2)}) collective-permute-start(bf16[32,6,1,128]{3,0,2,1:T(8,128)(2,1)S(1)} %get-tuple-element.18), channel_id=1, source_target_pairs={{0,4},{4,8},{8,12},{12,16},{16,20},{20,24},{24,28},{1,5},{5,9},{9,... | collective-permute-start | bytes 147464 | tf_op jit(solution)/shard_map/ppermute | solution.py:16
  160.0 1.3 collective-permute-start.15
  164.8 7.0 %collective-permute-done.15 = bf16[32,6,1,128]{3,0,2,1:T(8,128)(2,1)S(1)} collective-permute-done((bf16[32,6,1,128]{3,0,2,1:T(8,128)(2,1)S(1)}, bf16[32,6,1,128]{3,0,2,1:T(8,128)(2,1)S(1)}, u32[]{:S(2)}, u32[]{:S(2)}) %collective-permute-start.15) | collective-permute-done | bytes 49184 | tf_op jit(solution)/shard_map/ppermute | solution.py:18
  173.7 1.0 fusion.228
  175.6 1.0 fusion.232
  177.5 1.0 fusion.236
  179.5 1.0 fusion.242
  181.4 1.0 fusion.209
  183.3 1.0 fusion.215
  185.3 1.0 fusion.221
  187.2 1.0 fusion.203
  190.3 1.0 fusion.310
  192.3 1.1 fusion.316
  194.2 1.0 fusion.322
  196.1 1.1 fusion.328
  198.1 1.1 convolution_bitcast_fusion.11
  200.0 1.0 convolution_bitcast_fusion.13
  201.1 1.0 convolution_bitcast_fusion.7
  203.0 1.1 convolution_bitcast_fusion.9
  213.4 413.0 %all-reduce.4 = (f32[8,32,3,3,3]{1,0,4,3,2:T(8,128)}, f32[8]{0:T(128)S(1)}, f32[8,32,3,3,3]{1,0,4,3,2:T(8,128)}) all-reduce(f32[8,32,3,3,3]{1,0,4,3,2:T(8,128)} %bitcast.1393, f32[8]{0:T(128)S(1)} %get-tuple-element.50, f32[8,32,3,3,3]{1,0,4,3,2:T(8,128)} %bitcast.1394), channel_id=1, replica_groups=mesh['gx'=8,'gy'=8,'af'=4] {'gx','gy'}, use_global_device_ids=true, to_apply=%region_0.1 | all-reduce | flops 13832 | bytes 110656 | tf_op jit(solution)/shard_map/psum | solution.py:108
  627.0 1.4 fusion.187
  628.3 1.2 fusion.181
  631.6 1.0 fusion.178
  634.5 1.1 fusion.108
  636.4 1.0 fusion.411
  640.3 1.0 fusion.391
  643.1 1.1 fusion.109
  (309 shorter events, 66.1 us)
Async XLA Ops:
  0.6 38.1 %copy-start.50 = (bf16[8,32,3,3,3]{1,0,4,3,2:T(8,128)(2,1)S(1)}, bf16[8,32,3,3,3]{1,0,4,3,2:T(8,128)(2,1)}, u32[]{:S(2)}) copy-start(bf16[8,32,3,3,3]{1,0,4,3,2:T(8,128)(2,1)} %param.6) | copy-start | bytes 41476
  1.7 37.2 %copy-start.48 = (bf16[8,32,3,3,3]{1,0,4,3,2:T(8,128)(2,1)S(1)}, bf16[8,32,3,3,3]{1,0,4,3,2:T(8,128)(2,1)}, u32[]{:S(2)}) copy-start(bf16[8,32,3,3,3]{1,0,4,3,2:T(8,128)(2,1)} %param.8) | copy-start | bytes 41476
  16.3 49.2 %collective-permute-start = (bf16[32,1,16,128]{3,0,2,1:T(8,128)(2,1)S(1)}, bf16[32,1,16,128]{3,0,2,1:T(8,128)(2,1)S(1)}, u32[]{:S(2)}, u32[]{:S(2)}) collective-permute-start(bf16[32,1,16,128]{3,0,2,1:T(8,128)(2,1)S(1)} %get-tuple-element.39), channel_id=1, source_target_pairs={{0,32},{32,64},{64,96},{96,128},{128,160},{160,192},{192,224},{1,3... | collective-permute-start | bytes 393224 | tf_op jit(solution)/shard_map/ppermute | solution.py:16
  17.6 48.3 %collective-permute-start.1 = (bf16[32,1,16,128]{3,0,2,1:T(8,128)(2,1)S(1)}, bf16[32,1,16,128]{3,0,2,1:T(8,128)(2,1)S(1)}, u32[]{:S(2)}, u32[]{:S(2)}) collective-permute-start(bf16[32,1,16,128]{3,0,2,1:T(8,128)(2,1)S(1)} %get-tuple-element.38), channel_id=1, source_target_pairs={{32,0},{64,32},{96,64},{128,96},{160,128},{192,160},{224,192},{33,... | collective-permute-start | bytes 393224 | tf_op jit(solution)/shard_map/ppermute | solution.py:18
  35.2 35.8 %collective-permute-start.8 = (bf16[32,1,16,128]{3,0,2,1:T(8,128)(2,1)S(1)}, bf16[32,1,16,128]{3,0,2,1:T(8,128)(2,1)S(1)}, u32[]{:S(2)}, u32[]{:S(2)}) collective-permute-start(bf16[32,1,16,128]{3,0,2,1:T(8,128)(2,1)S(1)} %get-tuple-element.29), channel_id=1, source_target_pairs={{0,32},{32,64},{64,96},{96,128},{128,160},{160,192},{192,224},{1,3... | collective-permute-start | bytes 393224 | tf_op jit(solution)/shard_map/ppermute | solution.py:16
  37.4 33.8 %collective-permute-start.9 = (bf16[32,1,16,128]{3,0,2,1:T(8,128)(2,1)S(1)}, bf16[32,1,16,128]{3,0,2,1:T(8,128)(2,1)S(1)}, u32[]{:S(2)}, u32[]{:S(2)}) collective-permute-start(bf16[32,1,16,128]{3,0,2,1:T(8,128)(2,1)S(1)} %get-tuple-element.28), channel_id=1, source_target_pairs={{32,0},{64,32},{96,64},{128,96},{160,128},{192,160},{224,192},{33,... | collective-permute-start | bytes 393224 | tf_op jit(solution)/shard_map/ppermute | solution.py:18
  65.5 121.7 %copy-start.47 = (bf16[8,32,3,3,3]{1,0,4,3,2:T(8,128)(2,1)}, bf16[8,32,3,3,3]{1,0,4,3,2:T(8,128)(2,1)S(1)}, u32[]{:S(2)}) copy-start(bf16[8,32,3,3,3]{1,0,4,3,2:T(8,128)(2,1)S(1)} %dynamic-slice_bitcast_fusion.1) | copy-start | bytes 41476
  66.0 11.6 %collective-permute-start.2 = (bf16[32,6,1,128]{3,0,2,1:T(8,128)(2,1)S(1)}, bf16[32,6,1,128]{3,0,2,1:T(8,128)(2,1)S(1)}, u32[]{:S(2)}, u32[]{:S(2)}) collective-permute-start(bf16[32,6,1,128]{3,0,2,1:T(8,128)(2,1)S(1)} %get-tuple-element.24), channel_id=1, source_target_pairs={{0,4},{4,8},{8,12},{12,16},{16,20},{20,24},{24,28},{1,5},{5,9},{9,... | collective-permute-start | bytes 147464 | tf_op jit(solution)/shard_map/ppermute | solution.py:16
  69.4 8.3 %collective-permute-start.3 = (bf16[32,6,1,128]{3,0,2,1:T(8,128)(2,1)S(1)}, bf16[32,6,1,128]{3,0,2,1:T(8,128)(2,1)S(1)}, u32[]{:S(2)}, u32[]{:S(2)}) collective-permute-start(bf16[32,6,1,128]{3,0,2,1:T(8,128)(2,1)S(1)} %get-tuple-element.25), channel_id=1, source_target_pairs={{4,0},{8,4},{12,8},{16,12},{20,16},{24,20},{28,24},{5,1},{9,5},{13... | collective-permute-start | bytes 147464 | tf_op jit(solution)/shard_map/ppermute | solution.py:18
  71.2 11.8 %collective-permute-start.10 = (bf16[32,6,1,128]{3,0,2,1:T(8,128)(2,1)S(1)}, bf16[32,6,1,128]{3,0,2,1:T(8,128)(2,1)S(1)}, u32[]{:S(2)}, u32[]{:S(2)}) collective-permute-start(bf16[32,6,1,128]{3,0,2,1:T(8,128)(2,1)S(1)} %get-tuple-element.20), channel_id=1, source_target_pairs={{0,4},{4,8},{8,12},{12,16},{16,20},{20,24},{24,28},{1,5},{5,9},{9,... | collective-permute-start | bytes 147464 | tf_op jit(solution)/shard_map/ppermute | solution.py:16
  75.8 7.3 %collective-permute-start.11 = (bf16[32,6,1,128]{3,0,2,1:T(8,128)(2,1)S(1)}, bf16[32,6,1,128]{3,0,2,1:T(8,128)(2,1)S(1)}, u32[]{:S(2)}, u32[]{:S(2)}) collective-permute-start(bf16[32,6,1,128]{3,0,2,1:T(8,128)(2,1)S(1)} %get-tuple-element.21), channel_id=1, source_target_pairs={{4,0},{8,4},{12,8},{16,12},{20,16},{24,20},{28,24},{5,1},{9,5},{13... | collective-permute-start | bytes 147464 | tf_op jit(solution)/shard_map/ppermute | solution.py:18
  122.7 21.2 %collective-permute-start.4 = (bf16[32,1,16,128]{3,0,2,1:T(8,128)(2,1)S(1)}, bf16[32,1,16,128]{3,0,2,1:T(8,128)(2,1)S(1)}, u32[]{:S(2)}, u32[]{:S(2)}) collective-permute-start(bf16[32,1,16,128]{3,0,2,1:T(8,128)(2,1)S(1)} %get-tuple-element.34), channel_id=1, source_target_pairs={{0,32},{32,64},{64,96},{96,128},{128,160},{160,192},{192,224},{1,3... | collective-permute-start | bytes 393224 | tf_op jit(solution)/shard_map/ppermute | solution.py:16
  123.9 20.3 %collective-permute-start.5 = (bf16[32,1,16,128]{3,0,2,1:T(8,128)(2,1)S(1)}, bf16[32,1,16,128]{3,0,2,1:T(8,128)(2,1)S(1)}, u32[]{:S(2)}, u32[]{:S(2)}) collective-permute-start(bf16[32,1,16,128]{3,0,2,1:T(8,128)(2,1)S(1)} %get-tuple-element.33), channel_id=1, source_target_pairs={{32,0},{64,32},{96,64},{128,96},{160,128},{192,160},{224,192},{33,... | collective-permute-start | bytes 393224 | tf_op jit(solution)/shard_map/ppermute | solution.py:18
  132.2 17.8 %collective-permute-start.12 = (bf16[32,1,16,128]{3,0,2,1:T(8,128)(2,1)S(1)}, bf16[32,1,16,128]{3,0,2,1:T(8,128)(2,1)S(1)}, u32[]{:S(2)}, u32[]{:S(2)}) collective-permute-start(bf16[32,1,16,128]{3,0,2,1:T(8,128)(2,1)S(1)} %get-tuple-element.27), channel_id=1, source_target_pairs={{0,32},{32,64},{64,96},{96,128},{128,160},{160,192},{192,224},{1,3... | collective-permute-start | bytes 393224 | tf_op jit(solution)/shard_map/ppermute | solution.py:16
  141.1 9.1 %collective-permute-start.13 = (bf16[32,1,16,128]{3,0,2,1:T(8,128)(2,1)S(1)}, bf16[32,1,16,128]{3,0,2,1:T(8,128)(2,1)S(1)}, u32[]{:S(2)}, u32[]{:S(2)}) collective-permute-start(bf16[32,1,16,128]{3,0,2,1:T(8,128)(2,1)S(1)} %get-tuple-element.26), channel_id=1, source_target_pairs={{32,0},{64,32},{96,64},{128,96},{160,128},{192,160},{224,192},{33,... | collective-permute-start | bytes 393224 | tf_op jit(solution)/shard_map/ppermute | solution.py:18
  143.8 6.3 copy-start.51
  144.3 67.9 %copy-start.3 = (bf16[32,6,16,128]{3,0,2,1:T(8,128)(2,1)}, bf16[32,6,16,128]{3,0,2,1:T(8,128)(2,1)S(1)}, u32[]{:S(2)}) copy-start(bf16[32,6,16,128]{3,0,2,1:T(8,128)(2,1)S(1)} %get-tuple-element.43) | copy-start | bytes 2359300
  144.3 43.9 %collective-permute-start.6 = (bf16[32,6,1,128]{3,0,2,1:T(8,128)(2,1)S(1)}, bf16[32,6,1,128]{3,0,2,1:T(8,128)(2,1)S(1)}, u32[]{:S(2)}, u32[]{:S(2)}) collective-permute-start(bf16[32,6,1,128]{3,0,2,1:T(8,128)(2,1)S(1)} %get-tuple-element.22), channel_id=1, source_target_pairs={{0,4},{4,8},{8,12},{12,16},{16,20},{20,24},{24,28},{1,5},{5,9},{9,... | collective-permute-start | bytes 147464 | tf_op jit(solution)/shard_map/ppermute | solution.py:16
  148.7 39.5 %collective-permute-start.7 = (bf16[32,6,1,128]{3,0,2,1:T(8,128)(2,1)S(1)}, bf16[32,6,1,128]{3,0,2,1:T(8,128)(2,1)S(1)}, u32[]{:S(2)}, u32[]{:S(2)}) collective-permute-start(bf16[32,6,1,128]{3,0,2,1:T(8,128)(2,1)S(1)} %get-tuple-element.23), channel_id=1, source_target_pairs={{4,0},{8,4},{12,8},{16,12},{20,16},{24,20},{28,24},{5,1},{9,5},{13... | collective-permute-start | bytes 147464 | tf_op jit(solution)/shard_map/ppermute | solution.py:18
  150.2 21.7 %copy-start = (bf16[32,6,16,128]{3,0,2,1:T(8,128)(2,1)}, bf16[32,6,16,128]{3,0,2,1:T(8,128)(2,1)S(1)}, u32[]{:S(2)}) copy-start(bf16[32,6,16,128]{3,0,2,1:T(8,128)(2,1)S(1)} %constant_dynamic-update-slice_fusion.17) | copy-start | bytes 2359300
  150.2 14.6 %collective-permute-start.14 = (bf16[32,6,1,128]{3,0,2,1:T(8,128)(2,1)S(1)}, bf16[32,6,1,128]{3,0,2,1:T(8,128)(2,1)S(1)}, u32[]{:S(2)}, u32[]{:S(2)}) collective-permute-start(bf16[32,6,1,128]{3,0,2,1:T(8,128)(2,1)S(1)} %get-tuple-element.18), channel_id=1, source_target_pairs={{0,4},{4,8},{8,12},{12,16},{16,20},{20,24},{24,28},{1,5},{5,9},{9,... | collective-permute-start | bytes 147464 | tf_op jit(solution)/shard_map/ppermute | solution.py:16
  160.0 11.9 %collective-permute-start.15 = (bf16[32,6,1,128]{3,0,2,1:T(8,128)(2,1)S(1)}, bf16[32,6,1,128]{3,0,2,1:T(8,128)(2,1)S(1)}, u32[]{:S(2)}, u32[]{:S(2)}) collective-permute-start(bf16[32,6,1,128]{3,0,2,1:T(8,128)(2,1)S(1)} %get-tuple-element.19), channel_id=1, source_target_pairs={{4,0},{8,4},{12,8},{16,12},{20,16},{24,20},{28,24},{5,1},{9,5},{13... | collective-permute-start | bytes 147464 | tf_op jit(solution)/shard_map/ppermute | solution.py:18
  164.8 9.9 %copy-start.43 = (bf16[32,6,1,128]{3,0,2,1:T(8,128)(2,1)}, bf16[32,6,1,128]{3,0,2,1:T(8,128)(2,1)S(1)}, u32[]{:S(2)}) copy-start(bf16[32,6,1,128]{3,0,2,1:T(8,128)(2,1)S(1)} %collective-permute-done.14) | copy-start | bytes 147460
  188.3 21.9 %copy-start.55 = (bf16[32,6,1,128]{3,0,2,1:T(8,128)(2,1)}, bf16[32,6,1,128]{3,0,2,1:T(8,128)(2,1)S(1)}, u32[]{:S(2)}) copy-start(bf16[32,6,1,128]{3,0,2,1:T(8,128)(2,1)S(1)} %collective-permute-done.6) | copy-start | bytes 147460
  188.3 23.9 %copy-start.57 = (bf16[32,6,1,128]{3,0,2,1:T(8,128)(2,1)}, bf16[32,6,1,128]{3,0,2,1:T(8,128)(2,1)S(1)}, u32[]{:S(2)}) copy-start(bf16[32,6,1,128]{3,0,2,1:T(8,128)(2,1)S(1)} %collective-permute-done.7) | copy-start | bytes 147460
  626.4 3.2 copy-start.1
  626.4 3.2 copy-start.44
  626.9 3.6 copy-start.24
  626.9 3.6 copy-start.34
  626.9 3.6 copy-start.35
  626.9 3.6 copy-start.36
  626.9 3.6 copy-start.37
  626.9 3.6 copy-start.38
  626.9 3.6 copy-start.39
  626.9 3.6 copy-start.40
  627.0 3.6 copy-start.41
  627.0 3.6 copy-start.42
  634.5 2.9 copy-start.58
  636.3 2.8 copy-start.23
  636.3 2.8 copy-start.25
  636.3 2.9 copy-start.26
  636.3 2.9 copy-start.27
  636.3 2.9 copy-start.28
  636.3 2.9 copy-start.29
  636.3 2.9 copy-start.30
  636.3 2.9 copy-start.31
  636.3 2.9 copy-start.32
  636.4 2.9 copy-start.33
  (28 other events, 66.5 us)
where the time goes:
time: 647 us; the launch traced here: 646 us
  blocking collectives  499 us (77%)
  matrix products  80.8 us (12%)
  starting transfers between devices  46.4 us (7%)
  waiting for transfers between devices  7.08 us (1%)
    psum x1, blocking collectives, body(): lax.psum((local_one, local_bias, local_two), ('gx', 'gy'))  413 us
    dot_general x108, matrix products, conv_valid(): jnp.einsum('oi,ixyz->oxyz', weight[:, :, off_x, off_y, off_z], window, pr...  65.3 us
    all_gather x4, blocking collectives, full_padded(): gathered = lax.all_gather(values, 'af', axis=0, tiled=True)  59.7 us
    ppermute x8, starting transfers between devices, with_halo(): lax.ppermute(tail, axis, [(i, (i + 1) % count) for i in range(ends)])  35.7 us
    dot_general x54, matrix products, kernel_grad(): jnp.einsum('oxyz,ixyz->oi', cot_field, window, preferred_element_type=jnp...  15.6 us
    all_gather x1, blocking collectives, body(): lax.all_gather(weight_one, 'af', axis=0, tiled=True)  13 us
    all_gather x1, blocking collectives, body(): lax.all_gather(weight_two, 'af', axis=0, tiled=True)  13 us
  transfers between devices with their start and end apart: 16, of which 1 were waited for; matrix products, arithmetic and copies ran while one was open for 6% of the time, Pallas kernels for 0%

commit v1 on v0

--- a/solution.py
+++ b/solution.py
@@ -71,7 +71,15 @@
 
 
 def full_padded(values):
-    gathered = lax.all_gather(values, "af", axis=0, tiled=True)
+    gathered = jnp.concatenate(
+        lax.all_to_all(
+            jnp.stack([values for _ in range(lax.psum(1, axis_name="af"))]),
+            axis_name="af",
+            split_axis=0,
+            concat_axis=0,
+        ),
+        0,
+    )
     rimmed = with_halo(gathered, (("gx", 1), ("gy", 2)), 1)
     return depth_pad(rimmed)
 

time: 647 us -> 662 us (1.023)
  blocking collectives: 499 us -> 442 us
  starting transfers between devices: 46.4 us -> 70.3 us
  waiting for transfers between devices: 7.08 us -> 26.1 us
  matrix products: 80.8 us -> 99.3 us
    all_gather x4 -> x0, blocking collectives: 59.7 us -> none  [full_padded(): gathered = lax.all_gather(values, 'af', axis=0, tiled=True)]
    all_to_all x0 -> x4, starting transfers between devices: none -> 26.1 us  [full_padded(): lax.all_to_all(jnp.stack([values for _ in range(lax.psum(1, axis_name='af...]
    all_to_all x0 -> x4, waiting for transfers between devices: none -> 22.3 us  [full_padded(): lax.all_to_all(jnp.stack([values for _ in range(lax.psum(1, axis_name='af...]
    dot_general x54, matrix products: 15.6 us -> 32.3 us  [kernel_grad(): jnp.einsum('oxyz,ixyz->oi', cot_field, window, preferred_element_type=jnp...]
    all_gather x1, blocking collectives: 13 us -> 20.5 us  [body(): lax.all_gather(weight_one, 'af', axis=0, tiled=True)]
  transfers between devices with their start and end apart: 16 -> 20, of which waited for: 1 -> 4; matrix products, arithmetic and copies ran while one was open for 6% -> 8% of each run, Pallas kernels for 0% -> 0%
where the time goes in v1:
time: 662 us; the launch traced here: 659 us
  blocking collectives  442 us (67%)
  matrix products  99.3 us (15%)
  starting transfers between devices  70.3 us (11%)
  waiting for transfers between devices  26.1 us (4%)
  local copies, waits for them, and re-layouts  10 us (2%)
  other arithmetic  8.79 us (1%)
    psum x1, blocking collectives, body(): lax.psum((local_one, local_bias, local_two), ('gx', 'gy'))  409 us
    dot_general x108, matrix products, conv_valid(): jnp.einsum('oi,ixyz->oxyz', weight[:, :, off_x, off_y, off_z], window, pr...  67 us
    ppermute x8, starting transfers between devices, with_halo(): lax.ppermute(tail, axis, [(i, (i + 1) % count) for i in range(ends)])  33.5 us
    dot_general x54, matrix products, kernel_grad(): jnp.einsum('oxyz,ixyz->oi', cot_field, window, preferred_element_type=jnp...  32.3 us
    all_to_all x4, starting transfers between devices, full_padded(): lax.all_to_all(jnp.stack([values for _ in range(lax.psum(1, axis_name='af...  26.1 us
    all_to_all x4, waiting for transfers between devices, full_padded(): lax.all_to_all(jnp.stack([values for _ in range(lax.psum(1, axis_name='af...  22.3 us
    all_gather x1, blocking collectives, body(): lax.all_gather(weight_one, 'af', axis=0, tiled=True)  20.5 us
  transfers between devices with their start and end apart: 20, of which 4 were waited for; matrix products, arithmetic and copies ran while one was open for 8% of the time, Pallas kernels for 0%

profile of v1, /device:TPU:0, one launch (start us, length us, event | category | flops | bytes accessed | tf_op | source)
XLA Modules:
  0.0 658.8 jit_solution(257554315714373793)
XLA Ops:
  2.6 4.2 all-to-all-start.2
  6.8 14.4 %all-to-all-done.2 = bf16[4,8,4,16,128]{4,1,3,2,0:T(8,128)(2,1)S(1)} async-done(((bf16[4,8,4,16,128]{4,1,3,2,0:T(8,128)(2,1)}), bf16[4,8,4,16,128]{4,1,3,2,0:T(8,128)(2,1)S(1)}, u32[]{:S(2)}, u32[]{:S(2)}) %all-to-all-start.2) | async-done | bytes 524320 | tf_op jit(solution)/shard_map/all_to_all | solution.py:75
  22.1 3.5 all-to-all-start
  25.6 20.5 %all_gather.6 = bf16[32,32,3,3,3]{1,0,4,3,2:T(8,128)(2,1)S(1)} all-gather(bf16[8,32,3,3,3]{1,0,4,3,2:T(8,128)(2,1)S(1)} %copy-done.50), channel_id=1, replica_groups=mesh['gx'=8,'gy'=8,'af'=4] {'af'}, dimensions={0}, use_global_device_ids=true | all-gather | bytes 69120 | tf_op jit(solution)/shard_map/all_gather | solution.py:101
  46.4 12.8 %all_gather.7 = bf16[32,32,3,3,3]{1,0,4,3,2:T(8,128)(2,1)S(1)} all-gather(bf16[8,32,3,3,3]{1,0,4,3,2:T(8,128)(2,1)S(1)} %copy-done.48), channel_id=1, replica_groups=mesh['gx'=8,'gy'=8,'af'=4] {'af'}, dimensions={0}, use_global_device_ids=true | all-gather | bytes 69120 | tf_op jit(solution)/shard_map/all_gather | solution.py:102
  60.1 1.3 collective-permute-start.8
  61.4 1.3 collective-permute-start.9
  62.9 4.8 collective-permute-start
  67.8 1.3 collective-permute-start.1
  70.2 3.4 collective-permute-start.10
  73.6 1.3 collective-permute-start.11
  75.0 4.5 collective-permute-start.2
  79.5 1.7 collective-permute-start.3
  83.3 2.2 collective-permute-done.3
  87.0 1.7 fusion.10
  98.8 1.7 select_maximum_fusion.4
  100.5 1.1 fusion.247
  101.5 1.1 fusion.249
  103.6 1.0 fusion.255
  105.5 1.0 fusion.261
  110.2 1.0 fusion.276
  112.2 1.0 fusion.282
  115.1 1.0 fusion.243
  116.2 1.8 multiply_convert_fusion
  118.9 13.6 %all-to-all-start.1 = ((bf16[4,8,4,16,128]{4,1,3,2,0:T(8,128)(2,1)}), bf16[4,8,4,16,128]{4,1,3,2,0:T(8,128)(2,1)}, u32[]{:S(2)}, u32[]{:S(2)}) async-start(bf16[4,8,4,16,128]{4,1,3,2,0:T(8,128)(2,1)} %stack.197), calls=%async_computation.1 | async-start | bytes 1048576 | tf_op jit(solution)/shard_map/all_to_all | solution.py:75
  132.7 2.3 fusion.81
  135.5 1.8 convert_reduce_fusion
  159.2 4.8 all-to-all-start.3
  166.7 1.1 copy.308
  167.9 1.7 collective-permute-start.4
  169.6 1.3 collective-permute-start.5
  170.9 7.9 %all-to-all-done.3 = bf16[4,8,4,16,128]{4,1,3,2,0:T(8,128)(2,1)S(1)} async-done(((bf16[4,8,4,16,128]{4,1,3,2,0:T(8,128)(2,1)}), bf16[4,8,4,16,128]{4,1,3,2,0:T(8,128)(2,1)S(1)}, u32[]{:S(2)}, u32[]{:S(2)}) %all-to-all-start.3) | async-done | bytes 524320 | tf_op jit(solution)/shard_map/all_to_all | solution.py:75
  178.9 1.3 collective-permute-start.12
  180.2 1.3 collective-permute-start.13
  181.5 1.2 fusion.399
  183.7 6.3 collective-permute-start.6
  190.0 1.3 collective-permute-start.7
  191.3 10.1 %collective-permute-start.14 = (bf16[32,6,1,128]{3,0,2,1:T(8,128)(2,1)S(1)}, bf16[32,6,1,128]{3,0,2,1:T(8,128)(2,1)S(1)}, u32[]{:S(2)}, u32[]{:S(2)}) collective-permute-start(bf16[32,6,1,128]{3,0,2,1:T(8,128)(2,1)S(1)} %get-tuple-element.20), channel_id=1, source_target_pairs={{0,4},{4,8},{8,12},{12,16},{16,20},{20,24},{24,28},{1,5},{5,9},{9,... | collective-permute-start | bytes 147464 | tf_op jit(solution)/shard_map/ppermute | solution.py:16
  201.4 1.3 collective-permute-start.15
  205.5 1.7 select_maximum_fusion.8
  211.6 1.6 collective-permute-done.15
  217.3 1.8 select_maximum_fusion
  223.9 1.0 fusion.211
  226.7 1.1 fusion.220
  228.6 1.0 fusion.226
  238.0 1.3 fusion.137
  244.8 409.1 %all-reduce.4 = (f32[8,32,3,3,3]{1,0,4,3,2:T(8,128)S(1)}, f32[8]{0:T(128)S(1)}, f32[8,32,3,3,3]{1,0,4,3,2:T(8,128)S(1)}) all-reduce(f32[8,32,3,3,3]{1,0,4,3,2:T(8,128)} %bitcast.436, f32[8]{0:T(128)S(1)} %get-tuple-element.44, f32[8,32,3,3,3]{1,0,4,3,2:T(8,128)} %bitcast.1445), channel_id=1, replica_groups=mesh['gx'=8,'gy'=8,'af'=4] {'gx','gy'}, use_global_device_ids=true, to_apply=%region_0.1 | all-reduce | flops 13832 | bytes 110656 | tf_op jit(solution)/shard_map/psum | solution.py:116
  654.5 2.1 fusion.105
  (301 shorter events, 89.0 us)
Async XLA Ops:
  0.6 6.1 copy-start.51
  1.7 23.9 %copy-start.50 = (bf16[8,32,3,3,3]{1,0,4,3,2:T(8,128)(2,1)S(1)}, bf16[8,32,3,3,3]{1,0,4,3,2:T(8,128)(2,1)}, u32[]{:S(2)}) copy-start(bf16[8,32,3,3,3]{1,0,4,3,2:T(8,128)(2,1)} %param.6) | copy-start | bytes 41476
  2.6 18.6 %all-to-all-start.2 = ((bf16[4,8,4,16,128]{4,1,3,2,0:T(8,128)(2,1)}), bf16[4,8,4,16,128]{4,1,3,2,0:T(8,128)(2,1)S(1)}, u32[]{:S(2)}, u32[]{:S(2)}) async-start(bf16[4,8,4,16,128]{4,1,3,2,0:T(8,128)(2,1)} %stack.198), calls=%async_computation.2 | async-start | bytes 1048576 | tf_op jit(solution)/shard_map/all_to_all | solution.py:75
  6.7 39.6 %copy-start.48 = (bf16[8,32,3,3,3]{1,0,4,3,2:T(8,128)(2,1)S(1)}, bf16[8,32,3,3,3]{1,0,4,3,2:T(8,128)(2,1)}, u32[]{:S(2)}) copy-start(bf16[8,32,3,3,3]{1,0,4,3,2:T(8,128)(2,1)} %param.8) | copy-start | bytes 41476
  22.1 40.6 %all-to-all-start = ((bf16[4,8,4,16,128]{4,1,3,2,0:T(8,128)(2,1)}), bf16[4,8,4,16,128]{4,1,3,2,0:T(8,128)(2,1)S(1)}, u32[]{:S(2)}, u32[]{:S(2)}) async-start(bf16[4,8,4,16,128]{4,1,3,2,0:T(8,128)(2,1)} %stack.196), calls=%async_computation | async-start | bytes 1048576 | tf_op jit(solution)/shard_map/all_to_all | solution.py:75
  60.0 37.9 %copy-start.46 = (bf16[8,32,3,3,3]{1,0,4,3,2:T(8,128)(2,1)}, bf16[8,32,3,3,3]{1,0,4,3,2:T(8,128)(2,1)S(1)}, u32[]{:S(2)}) copy-start(bf16[8,32,3,3,3]{1,0,4,3,2:T(8,128)(2,1)S(1)} %dynamic-slice_bitcast_fusion) | copy-start | bytes 41476
  60.1 33.1 %copy-start.5 = (bf16[4,8,4,16,128]{4,1,0,3,2:T(8,128)(2,1)}, bf16[4,8,4,16,128]{4,1,0,3,2:T(8,128)(2,1)S(1)}, u32[]{:S(2)}) copy-start(bf16[4,8,4,16,128]{4,1,0,3,2:T(8,128)(2,1)S(1)} %copy.307) | copy-start | bytes 1572868
  60.1 10.0 %collective-permute-start.8 = (bf16[32,1,16,128]{3,0,2,1:T(8,128)(2,1)S(1)}, bf16[32,1,16,128]{3,0,2,1:T(8,128)(2,1)S(1)}, u32[]{:S(2)}, u32[]{:S(2)}) collective-permute-start(bf16[32,1,16,128]{3,0,2,1:T(8,128)(2,1)S(1)} %get-tuple-element.36), channel_id=1, source_target_pairs={{0,32},{32,64},{64,96},{96,128},{128,160},{160,192},{192,224},{1,3... | collective-permute-start | bytes 393224 | tf_op jit(solution)/shard_map/ppermute | solution.py:16
  61.4 8.7 %collective-permute-start.9 = (bf16[32,1,16,128]{3,0,2,1:T(8,128)(2,1)S(1)}, bf16[32,1,16,128]{3,0,2,1:T(8,128)(2,1)S(1)}, u32[]{:S(2)}, u32[]{:S(2)}) collective-permute-start(bf16[32,1,16,128]{3,0,2,1:T(8,128)(2,1)S(1)} %get-tuple-element.37), channel_id=1, source_target_pairs={{32,0},{64,32},{96,64},{128,96},{160,128},{192,160},{224,192},{33,... | collective-permute-start | bytes 393224 | tf_op jit(solution)/shard_map/ppermute | solution.py:18
  62.8 7.4 %copy-start.9 = (bf16[4,8,4,16,128]{4,1,3,2,0:T(8,128)(2,1)}, bf16[4,8,4,16,128]{4,1,3,2,0:T(8,128)(2,1)S(1)}, u32[]{:S(2)}) copy-start(bf16[4,8,4,16,128]{4,1,3,2,0:T(8,128)(2,1)S(1)} %all-to-all-done) | copy-start | bytes 1572868
  62.9 24.1 %copy-start.7 = (bf16[4,8,4,16,128]{4,1,0,3,2:T(8,128)(2,1)}, bf16[4,8,4,16,128]{4,1,0,3,2:T(8,128)(2,1)S(1)}, u32[]{:S(2)}) copy-start(bf16[4,8,4,16,128]{4,1,0,3,2:T(8,128)(2,1)S(1)} %copy.309) | copy-start | bytes 1572868
  62.9 12.0 %collective-permute-start = (bf16[32,1,16,128]{3,0,2,1:T(8,128)(2,1)S(1)}, bf16[32,1,16,128]{3,0,2,1:T(8,128)(2,1)S(1)}, u32[]{:S(2)}, u32[]{:S(2)}) collective-permute-start(bf16[32,1,16,128]{3,0,2,1:T(8,128)(2,1)S(1)} %get-tuple-element.40), channel_id=1, source_target_pairs={{0,32},{32,64},{64,96},{96,128},{128,160},{160,192},{192,224},{1,3... | collective-permute-start | bytes 393224 | tf_op jit(solution)/shard_map/ppermute | solution.py:16
  67.8 7.2 %collective-permute-start.1 = (bf16[32,1,16,128]{3,0,2,1:T(8,128)(2,1)S(1)}, bf16[32,1,16,128]{3,0,2,1:T(8,128)(2,1)S(1)}, u32[]{:S(2)}, u32[]{:S(2)}) collective-permute-start(bf16[32,1,16,128]{3,0,2,1:T(8,128)(2,1)S(1)} %get-tuple-element.41), channel_id=1, source_target_pairs={{32,0},{64,32},{96,64},{128,96},{160,128},{192,160},{224,192},{33,... | collective-permute-start | bytes 393224 | tf_op jit(solution)/shard_map/ppermute | solution.py:18
  70.1 23.1 %copy-start.12 = (bf16[32,1,16,128]{3,0,2,1:T(8,128)(2,1)}, bf16[32,1,16,128]{3,0,2,1:T(8,128)(2,1)S(1)}, u32[]{:S(2)}) copy-start(bf16[32,1,16,128]{3,0,2,1:T(8,128)(2,1)S(1)} %collective-permute-done.8) | copy-start | bytes 393220
  70.2 23.1 %copy-start.14 = (bf16[32,1,16,128]{3,0,2,1:T(8,128)(2,1)}, bf16[32,1,16,128]{3,0,2,1:T(8,128)(2,1)S(1)}, u32[]{:S(2)}) copy-start(bf16[32,1,16,128]{3,0,2,1:T(8,128)(2,1)S(1)} %collective-permute-done.9) | copy-start | bytes 393220
  70.2 23.0 %collective-permute-start.10 = (bf16[32,6,1,128]{3,0,2,1:T(8,128)(2,1)S(1)}, bf16[32,6,1,128]{3,0,2,1:T(8,128)(2,1)S(1)}, u32[]{:S(2)}, u32[]{:S(2)}) collective-permute-start(bf16[32,6,1,128]{3,0,2,1:T(8,128)(2,1)S(1)} %get-tuple-element.24), channel_id=1, source_target_pairs={{0,4},{4,8},{8,12},{12,16},{16,20},{20,24},{24,28},{1,5},{5,9},{9,... | collective-permute-start | bytes 147464 | tf_op jit(solution)/shard_map/ppermute | solution.py:16
  73.6 19.6 %collective-permute-start.11 = (bf16[32,6,1,128]{3,0,2,1:T(8,128)(2,1)S(1)}, bf16[32,6,1,128]{3,0,2,1:T(8,128)(2,1)S(1)}, u32[]{:S(2)}, u32[]{:S(2)}) collective-permute-start(bf16[32,6,1,128]{3,0,2,1:T(8,128)(2,1)S(1)} %get-tuple-element.25), channel_id=1, source_target_pairs={{4,0},{8,4},{12,8},{16,12},{20,16},{24,20},{28,24},{5,1},{9,5},{13... | collective-permute-start | bytes 147464 | tf_op jit(solution)/shard_map/ppermute | solution.py:18
  74.9 12.1 %copy-start.18 = (bf16[32,1,16,128]{3,0,2,1:T(8,128)(2,1)}, bf16[32,1,16,128]{3,0,2,1:T(8,128)(2,1)S(1)}, u32[]{:S(2)}) copy-start(bf16[32,1,16,128]{3,0,2,1:T(8,128)(2,1)S(1)} %collective-permute-done) | copy-start | bytes 393220
  74.9 12.1 %copy-start.16 = (bf16[32,1,16,128]{3,0,2,1:T(8,128)(2,1)}, bf16[32,1,16,128]{3,0,2,1:T(8,128)(2,1)S(1)}, u32[]{:S(2)}) copy-start(bf16[32,1,16,128]{3,0,2,1:T(8,128)(2,1)S(1)} %collective-permute-done.1) | copy-start | bytes 393220
  75.0 8.4 %collective-permute-start.2 = (bf16[32,6,1,128]{3,0,2,1:T(8,128)(2,1)S(1)}, bf16[32,6,1,128]{3,0,2,1:T(8,128)(2,1)S(1)}, u32[]{:S(2)}, u32[]{:S(2)}) collective-permute-start(bf16[32,6,1,128]{3,0,2,1:T(8,128)(2,1)S(1)} %get-tuple-element.32), channel_id=1, source_target_pairs={{0,4},{4,8},{8,12},{12,16},{16,20},{20,24},{24,28},{1,5},{5,9},{9,... | collective-permute-start | bytes 147464 | tf_op jit(solution)/shard_map/ppermute | solution.py:16
  79.5 6.0 collective-permute-start.3
  95.2 3.6 copy-start.6
  95.2 3.6 copy-start.13
  95.2 3.6 copy-start.15
  100.5 32.1 %copy-start = (bf16[32,6,18,130]{3,0,2,1:T(8,128)(2,1)}, bf16[32,6,18,130]{3,0,2,1:T(8,128)(2,1)S(1)}, u32[]{:S(2)}) copy-start(bf16[32,6,18,130]{3,0,2,1:T(8,128)(2,1)S(1)} %select_maximum_fusion.4) | copy-start | bytes 2695684
  112.2 4.0 copy-start.53
  118.9 39.4 %all-to-all-start.1 = ((bf16[4,8,4,16,128]{4,1,3,2,0:T(8,128)(2,1)}), bf16[4,8,4,16,128]{4,1,3,2,0:T(8,128)(2,1)}, u32[]{:S(2)}, u32[]{:S(2)}) async-start(bf16[4,8,4,16,128]{4,1,3,2,0:T(8,128)(2,1)} %stack.197), calls=%async_computation.1 | async-start | bytes 1048576 | tf_op jit(solution)/shard_map/all_to_all | solution.py:75
  132.7 2.8 copy-start.41
  132.7 2.8 copy-start.42
  135.5 2.7 copy-start.4
  137.4 3.5 copy-start.8
  137.4 3.5 copy-start.19
  139.1 4.4 copy-start.2
  144.3 4.4 copy-start.10
  152.2 4.4 copy-start.17
  159.2 19.6 %all-to-all-start.3 = ((bf16[4,8,4,16,128]{4,1,3,2,0:T(8,128)(2,1)}), bf16[4,8,4,16,128]{4,1,3,2,0:T(8,128)(2,1)S(1)}, u32[]{:S(2)}, u32[]{:S(2)}) async-start(bf16[4,8,4,16,128]{4,1,3,2,0:T(8,128)(2,1)} %stack.199), calls=%async_computation.3 | async-start | bytes 1048576 | tf_op jit(solution)/shard_map/all_to_all | solution.py:75
  165.8 15.8 %copy-start.49 = (bf16[8,32,3,3,3]{1,0,4,3,2:T(8,128)(2,1)S(1)}, bf16[8,32,3,3,3]{1,0,4,3,2:T(8,128)(2,1)}, u32[]{:S(2)}) copy-start(bf16[8,32,3,3,3]{1,0,4,3,2:T(8,128)(2,1)} %param.8) | copy-start | bytes 41476
  166.7 16.1 %copy-start.45 = (bf16[8,32,3,3,3]{1,0,4,3,2:T(8,128)(2,1)S(1)}, bf16[8,32,3,3,3]{1,0,4,3,2:T(8,128)(2,1)}, u32[]{:S(2)}) copy-start(bf16[8,32,3,3,3]{1,0,4,3,2:T(8,128)(2,1)} %dynamic-slice_bitcast_fusion.1) | copy-start | bytes 41476
  167.9 15.8 %collective-permute-start.4 = (bf16[32,1,16,128]{3,0,2,1:T(8,128)(2,1)S(1)}, bf16[32,1,16,128]{3,0,2,1:T(8,128)(2,1)S(1)}, u32[]{:S(2)}, u32[]{:S(2)}) collective-permute-start(bf16[32,1,16,128]{3,0,2,1:T(8,128)(2,1)S(1)} %get-tuple-element.38), channel_id=1, source_target_pairs={{0,32},{32,64},{64,96},{96,128},{128,160},{160,192},{192,224},{1,3... | collective-permute-start | bytes 393224 | tf_op jit(solution)/shard_map/ppermute | solution.py:16
  169.6 14.1 %collective-permute-start.5 = (bf16[32,1,16,128]{3,0,2,1:T(8,128)(2,1)S(1)}, bf16[32,1,16,128]{3,0,2,1:T(8,128)(2,1)S(1)}, u32[]{:S(2)}, u32[]{:S(2)}) collective-permute-start(bf16[32,1,16,128]{3,0,2,1:T(8,128)(2,1)S(1)} %get-tuple-element.39), channel_id=1, source_target_pairs={{32,0},{64,32},{96,64},{128,96},{160,128},{192,160},{224,192},{33,... | collective-permute-start | bytes 393224 | tf_op jit(solution)/shard_map/ppermute | solution.py:18
  178.9 12.3 %collective-permute-start.12 = (bf16[32,1,16,128]{3,0,2,1:T(8,128)(2,1)S(1)}, bf16[32,1,16,128]{3,0,2,1:T(8,128)(2,1)S(1)}, u32[]{:S(2)}, u32[]{:S(2)}) collective-permute-start(bf16[32,1,16,128]{3,0,2,1:T(8,128)(2,1)S(1)} %get-tuple-element.34), channel_id=1, source_target_pairs={{0,32},{32,64},{64,96},{96,128},{128,160},{160,192},{192,224},{1,3... | collective-permute-start | bytes 393224 | tf_op jit(solution)/shard_map/ppermute | solution.py:16
  180.2 11.0 %collective-permute-start.13 = (bf16[32,1,16,128]{3,0,2,1:T(8,128)(2,1)S(1)}, bf16[32,1,16,128]{3,0,2,1:T(8,128)(2,1)S(1)}, u32[]{:S(2)}, u32[]{:S(2)}) collective-permute-start(bf16[32,1,16,128]{3,0,2,1:T(8,128)(2,1)S(1)} %get-tuple-element.35), channel_id=1, source_target_pairs={{32,0},{64,32},{96,64},{128,96},{160,128},{192,160},{224,192},{33,... | collective-permute-start | bytes 393224 | tf_op jit(solution)/shard_map/ppermute | solution.py:18
  183.7 20.5 %collective-permute-start.6 = (bf16[32,6,1,128]{3,0,2,1:T(8,128)(2,1)S(1)}, bf16[32,6,1,128]{3,0,2,1:T(8,128)(2,1)S(1)}, u32[]{:S(2)}, u32[]{:S(2)}) collective-permute-start(bf16[32,6,1,128]{3,0,2,1:T(8,128)(2,1)S(1)} %get-tuple-element.28), channel_id=1, source_target_pairs={{0,4},{4,8},{8,12},{12,16},{16,20},{20,24},{24,28},{1,5},{5,9},{9,... | collective-permute-start | bytes 147464 | tf_op jit(solution)/shard_map/ppermute | solution.py:16
  190.0 14.2 %collective-permute-start.7 = (bf16[32,6,1,128]{3,0,2,1:T(8,128)(2,1)S(1)}, bf16[32,6,1,128]{3,0,2,1:T(8,128)(2,1)S(1)}, u32[]{:S(2)}, u32[]{:S(2)}) collective-permute-start(bf16[32,6,1,128]{3,0,2,1:T(8,128)(2,1)S(1)} %get-tuple-element.29), channel_id=1, source_target_pairs={{4,0},{8,4},{12,8},{16,12},{20,16},{24,20},{28,24},{5,1},{9,5},{13... | collective-permute-start | bytes 147464 | tf_op jit(solution)/shard_map/ppermute | solution.py:18
  191.3 20.3 %collective-permute-start.14 = (bf16[32,6,1,128]{3,0,2,1:T(8,128)(2,1)S(1)}, bf16[32,6,1,128]{3,0,2,1:T(8,128)(2,1)S(1)}, u32[]{:S(2)}, u32[]{:S(2)}) collective-permute-start(bf16[32,6,1,128]{3,0,2,1:T(8,128)(2,1)S(1)} %get-tuple-element.20), channel_id=1, source_target_pairs={{0,4},{4,8},{8,12},{12,16},{16,20},{20,24},{24,28},{1,5},{5,9},{9,... | collective-permute-start | bytes 147464 | tf_op jit(solution)/shard_map/ppermute | solution.py:16
  201.4 11.7 %collective-permute-start.15 = (bf16[32,6,1,128]{3,0,2,1:T(8,128)(2,1)S(1)}, bf16[32,6,1,128]{3,0,2,1:T(8,128)(2,1)S(1)}, u32[]{:S(2)}, u32[]{:S(2)}) collective-permute-start(bf16[32,6,1,128]{3,0,2,1:T(8,128)(2,1)S(1)} %get-tuple-element.21), channel_id=1, source_target_pairs={{4,0},{8,4},{12,8},{16,12},{20,16},{24,20},{28,24},{5,1},{9,5},{13... | collective-permute-start | bytes 147464 | tf_op jit(solution)/shard_map/ppermute | solution.py:18
  243.7 410.7 %copy-start.43 = (f32[8,4,16,128]{3,0,2,1:T(8,128)S(1)}, f32[8,4,16,128]{3,0,2,1:T(8,128)}, u32[]{:S(2)}) copy-start(f32[8,4,16,128]{3,0,2,1:T(8,128)} %fusion.383) | copy-start | bytes 786436
  243.7 410.7 %copy-start.44 = (f32[8,4,16,128]{3,0,2,1:T(8,128)S(1)}, f32[8,4,16,128]{3,0,2,1:T(8,128)}, u32[]{:S(2)}) copy-start(f32[8,4,16,128]{3,0,2,1:T(8,128)} %fusion.234) | copy-start | bytes 786436
  (26 other events, 55.4 us)
